TPU v7x, 32 devices: a whole 2x2x4 slice. The times are simulated.
32 devices in a mesh: groups: 2 (over x), blk: 16 (over z, y, core).
Axes of the slice: x: 2, y: 2, z: 4, core: 2. Of those that a mesh axis runs over, the one named last changes fastest.
Arguments:
- samples: bfloat16 [64, 65536], P(None, ('groups', 'blk')), parts along dimension 1, may hold values from -6 to 6
- centre_index: int32 [32768], P(('groups', 'blk')), parts along dimension 0, may hold values from 0 to 32767, as said below
- probe_signs: int32 [32, 32768], P(None, ('groups', 'blk')), parts along dimension 1, may hold values from 0 to 1
- probe_scale: float32 [32768], P(('groups', 'blk')), parts along dimension 0, may hold values from 0.5 to 5
Outputs:
- product: float32 [32768, 32], P(('groups', 'blk')), parts along dimension 0
There are 2 independent parts, one for each index of `groups`. A program takes and returns all parts, laid end to end along the dimension named above; each array names one. Nothing has to cross between parts.
Inputs may be any that keep to these rules, and one draw needn't show every extreme that they name: `centre_index`: entry j names the sample serving as centre j. Within each aligned block of 1024 entries, at most 128 name samples of any one aligned block of 2048 samples, and in every such block of entries some block of samples is named exactly 128 times.
All inputs are finite; a program needn't handle non-finite values.
Results may differ from a plain program's by a relative error of at most 0.0031.
Values may be sent and summed in bfloat16 or wider, within the bound.
A program may use at most 64 MiB of HBM per device.

v0:
```python
import jax
import jax.numpy as jnp
from jax import lax
from jax.sharding import PartitionSpec as P


def kernel_block(points, point_sq, centres):
    centre_sq = jnp.sum(jnp.square(centres.astype(jnp.float32)), axis=0)
    cross = lax.dot_general(
        points, centres, (((0,), (0,)), ((), ())), preferred_element_type=jnp.float32
    )
    distance = point_sq[:, None] + centre_sq[None, :] - 2.0 * cross
    return jnp.exp(distance * (-2.0 / points.shape[0])).astype(jnp.bfloat16)


def block_span():
    return 1024


def split_columns(array, span):
    return jnp.moveaxis(array.reshape(array.shape[0], -1, span), 1, 0)


def local(samples, centre_index, probe_signs, probe_scale):
    blocks = lax.axis_size("blk")
    s_dev = samples.shape[1]
    m_dev = centre_index.shape[0]
    cap = 2 * m_dev // blocks
    owner = centre_index // s_dev
    owner_hot = (owner[:, None] == jnp.arange(blocks)[None, :]).astype(jnp.int32)
    position = jnp.sum((jnp.cumsum(owner_hot, axis=0) - 1) * owner_hot, axis=1)
    wanted = (
        jnp.zeros((blocks * cap,), jnp.int32).at[owner * cap + position].set(centre_index % s_dev)
    )
    asked = lax.all_to_all(wanted, "blk", split_axis=0, concat_axis=0, tiled=True)
    outgoing = jnp.take(samples, asked, axis=1)
    arrived = lax.all_to_all(outgoing, "blk", split_axis=1, concat_axis=1, tiled=True)
    centres = jnp.take(arrived, owner * cap + position, axis=1)
    probe = ((2 * probe_signs - 1).astype(jnp.float32) * probe_scale[None, :]).astype(jnp.bfloat16)
    point_sq = jnp.sum(jnp.square(samples.astype(jnp.float32)), axis=0)
    empty = jnp.zeros((probe.shape[0], s_dev), jnp.float32)
    centre_piece = lax.all_gather(centres, "blk", axis=1, tiled=True)
    probe_piece = lax.all_gather(probe, "blk", axis=1, tiled=True)
    span = block_span()

    def step(total, inputs):
        centre_cols, probe_cols = inputs
        kernel = kernel_block(samples, point_sq, centre_cols)
        return (
            total
            + lax.dot_general(
                probe_cols, kernel, (((1,), (1,)), ((), ())), preferred_element_type=jnp.float32
            ),
            None,
        )

    total, _ = lax.scan(
        step, empty, (split_columns(centre_piece, span), split_columns(probe_piece, span))
    )
    hidden = total.astype(jnp.bfloat16)
    piece = lax.all_gather(centres, "blk", axis=1, tiled=True)
    span = block_span()

    def single(centre_cols):
        kernel = kernel_block(samples, point_sq, centre_cols)
        return lax.dot_general(
            kernel, hidden, (((0,), (1,)), ((), ())), preferred_element_type=jnp.float32
        )

    terms = lax.map(single, split_columns(piece, span)).reshape(piece.shape[1], hidden.shape[0])
    summed = lax.psum_scatter(terms, "blk", scatter_dimension=0, tiled=True)
    return summed / float(s_dev * blocks)


def solution(mesh):
    in_specs = (
        P(None, ("groups", "blk")),
        P(("groups", "blk")),
        P(None, ("groups", "blk")),
        P(("groups", "blk")),
    )
    out_specs = P(("groups", "blk"), None)
    return jax.shard_map(local, mesh=mesh, in_specs=in_specs, out_specs=out_specs, check_vma=False)
```

profile of v0, /device:TPU:0, one launch (start us, length us, event | category | flops | bytes accessed | tf_op | source)
XLA Modules:
  0.0 359.0 jit_solution(10426960882151461342)
XLA Ops:
  8.8 4.5 %reduce-window.6 = s32[16,8,128]{2,1,0:T(8,128)S(1)} reduce-window(s32[16,8,128]{2,1,0:T(8,128)S(1)} %fusion.28, s32[]{:T(128)} %constant.94.clone.1), window={size=1x1x128 pad=0_0x0_0x127_0}, to_apply=%region_0.1 | reduce-window | flops 2080768 | bytes 131076 | tf_op jit(solution)/shard_map/reduce-window
  13.8 4.9 %scatter_custom_fusion = s32[2048]{0:T(1024)} fusion(s32[1024]{0:T(1024)S(1)} %get-tuple-element.129, s32[1024]{0:T(1024)S(1)} %get-tuple-element.130, s32[]{:T(128)} %constant.94.clone.1), kind=kCustom, calls=%fused_computation.50 | custom fusion | bytes 8196 | tf_op jit(solution)/shard_map/scatter | solution.py:33
  18.7 7.4 %all-to-all-start = ((s32[16,128,1]{1,2,0:T(1,128)}), s32[16,128,1]{1,2,0:T(1,128)S(1)}, u32[]{:S(2)}, u32[]{:S(2)}) async-start(s32[16,128,1]{1,2,0:T(1,128)} %bitcast.6), calls=%async_computation | async-start | bytes 16384 | tf_op jit(solution)/shard_map/all_to_all | solution.py:35
  27.3 5.2 %all-to-all-done = s32[16,128,1]{1,2,0:T(1,128)S(1)} async-done(((s32[16,128,1]{1,2,0:T(1,128)}), s32[16,128,1]{1,2,0:T(1,128)S(1)}, u32[]{:S(2)}, u32[]{:S(2)}) %all-to-all-start) | async-done | bytes 8224 | tf_op jit(solution)/shard_map/all_to_all | solution.py:35
  32.5 6.2 %gather_fusion = bf16[2048,64]{1,0:T(8,128)(2,1)S(1)} fusion(bf16[64,2048]{0,1:T(8,128)(2,1)S(1)} %copy.18, s32[2048]{0:T(1024)S(1)} %broadcast_clamp_fusion), kind=kCustom, calls=%fused_computation | custom fusion | bytes 532480 | tf_op jit(solution)/shard_map/jit(_take)/gather | solution.py:36
  39.7 3.5 all-to-all-start.1
  43.3 10.2 %all-to-all-done.1 = bf16[64,16,128]{2,0,1:T(8,128)(2,1)S(1)} async-done(((bf16[64,16,128]{2,0,1:T(8,128)(2,1)}), bf16[64,16,128]{2,0,1:T(8,128)(2,1)S(1)}, u32[]{:S(2)}, u32[]{:S(2)}) %all-to-all-start.1) | async-done | bytes 262176 | tf_op jit(solution)/shard_map/all_to_all | solution.py:37
  53.8 3.2 gather_fusion.1
  60.5 46.9 %all-gather.3.cloned.1.call-done = bf16[64,16384]{0,1:T(8,128)(2,1)} async-done(((bf16[64,1024]{0,1:T(8,128)(2,1)}), bf16[64,16384]{0,1:T(8,128)(2,1)}) %all-gather.3.cloned.1.call-update) | async-done | bytes 2097168 | tf_op jit(solution)/shard_map/all_gather | solution.py:61
  107.4 3.5 copy.21
  111.0 66.6 %while.22 = (s32[]{:T(128)}, f32[32,2048]{1,0:T(8,128)}, bf16[16,32,1024]{2,1,0:T(8,128)(2,1)S(1)}, f32[2048]{0:T(1024)S(1)}, bf16[16,64,1024]{2,1,0:T(8,128)(2,...) while((s32[]{:T(128)}, f32[32,2048]{1,0:T(8,128)}, ...), condition=%wide.region_7.8_spmd.clone, body=%wide.region_5.7_spmd.clone.sunk | while | flops 413465600 | bytes 1131619 | solution.py:57
  111.0 3.2 convolution_add_fusion.2
  114.3 4.2 %convolution_add_fusion.2 = f32[32,2048]{1,0:T(8,128)} fusion(bf16[64,2048]{1,0:T(8,128)(2,1)S(1)} %get-tuple-element.227, f32[1024]{0:T(1024)S(1)} %multiply_reduce_fusion.6, f32[2048]{0:T(1024)S(1)} %get-tuple-element.225, f32[32,2048]{1,0:T(8,128)} %get-tuple-element.215, pred[]{:T(512)S(6)} %compare.6, ...), kind=kOutput, calls=%fused_computation.19.clone.1 | convolution fusion | flops 413270016 | bytes 996353 | tf_op jit(solution)/shard_map/while/body/eval_jaxpr/dot_general | solution.py:51
  118.5 4.2 %convolution_add_fusion.2 = f32[32,2048]{1,0:T(8,128)} fusion(bf16[64,2048]{1,0:T(8,128)(2,1)S(1)} %get-tuple-element.227, f32[1024]{0:T(1024)S(1)} %multiply_reduce_fusion.6, f32[2048]{0:T(1024)S(1)} %get-tuple-element.225, f32[32,2048]{1,0:T(8,128)} %get-tuple-element.215, pred[]{:T(512)S(6)} %compare.6, ...), kind=kOutput, calls=%fused_computation.19.clone.1 | convolution fusion | flops 413270016 | bytes 996353 | tf_op jit(solution)/shard_map/while/body/eval_jaxpr/dot_general | solution.py:51
  122.7 4.2 %convolution_add_fusion.2 = f32[32,2048]{1,0:T(8,128)} fusion(bf16[64,2048]{1,0:T(8,128)(2,1)S(1)} %get-tuple-element.227, f32[1024]{0:T(1024)S(1)} %multiply_reduce_fusion.6, f32[2048]{0:T(1024)S(1)} %get-tuple-element.225, f32[32,2048]{1,0:T(8,128)} %get-tuple-element.215, pred[]{:T(512)S(6)} %compare.6, ...), kind=kOutput, calls=%fused_computation.19.clone.1 | convolution fusion | flops 413270016 | bytes 996353 | tf_op jit(solution)/shard_map/while/body/eval_jaxpr/dot_general | solution.py:51
  127.0 4.2 %convolution_add_fusion.2 = f32[32,2048]{1,0:T(8,128)} fusion(bf16[64,2048]{1,0:T(8,128)(2,1)S(1)} %get-tuple-element.227, f32[1024]{0:T(1024)S(1)} %multiply_reduce_fusion.6, f32[2048]{0:T(1024)S(1)} %get-tuple-element.225, f32[32,2048]{1,0:T(8,128)} %get-tuple-element.215, pred[]{:T(512)S(6)} %compare.6, ...), kind=kOutput, calls=%fused_computation.19.clone.1 | convolution fusion | flops 413270016 | bytes 996353 | tf_op jit(solution)/shard_map/while/body/eval_jaxpr/dot_general | solution.py:51
  131.2 4.2 %convolution_add_fusion.2 = f32[32,2048]{1,0:T(8,128)} fusion(bf16[64,2048]{1,0:T(8,128)(2,1)S(1)} %get-tuple-element.227, f32[1024]{0:T(1024)S(1)} %multiply_reduce_fusion.6, f32[2048]{0:T(1024)S(1)} %get-tuple-element.225, f32[32,2048]{1,0:T(8,128)} %get-tuple-element.215, pred[]{:T(512)S(6)} %compare.6, ...), kind=kOutput, calls=%fused_computation.19.clone.1 | convolution fusion | flops 413270016 | bytes 996353 | tf_op jit(solution)/shard_map/while/body/eval_jaxpr/dot_general | solution.py:51
  135.4 4.2 %convolution_add_fusion.2 = f32[32,2048]{1,0:T(8,128)} fusion(bf16[64,2048]{1,0:T(8,128)(2,1)S(1)} %get-tuple-element.227, f32[1024]{0:T(1024)S(1)} %multiply_reduce_fusion.6, f32[2048]{0:T(1024)S(1)} %get-tuple-element.225, f32[32,2048]{1,0:T(8,128)} %get-tuple-element.215, pred[]{:T(512)S(6)} %compare.6, ...), kind=kOutput, calls=%fused_computation.19.clone.1 | convolution fusion | flops 413270016 | bytes 996353 | tf_op jit(solution)/shard_map/while/body/eval_jaxpr/dot_general | solution.py:51
  139.6 4.2 %convolution_add_fusion.2 = f32[32,2048]{1,0:T(8,128)} fusion(bf16[64,2048]{1,0:T(8,128)(2,1)S(1)} %get-tuple-element.227, f32[1024]{0:T(1024)S(1)} %multiply_reduce_fusion.6, f32[2048]{0:T(1024)S(1)} %get-tuple-element.225, f32[32,2048]{1,0:T(8,128)} %get-tuple-element.215, pred[]{:T(512)S(6)} %compare.6, ...), kind=kOutput, calls=%fused_computation.19.clone.1 | convolution fusion | flops 413270016 | bytes 996353 | tf_op jit(solution)/shard_map/while/body/eval_jaxpr/dot_general | solution.py:51
  143.8 4.2 %convolution_add_fusion.2 = f32[32,2048]{1,0:T(8,128)} fusion(bf16[64,2048]{1,0:T(8,128)(2,1)S(1)} %get-tuple-element.227, f32[1024]{0:T(1024)S(1)} %multiply_reduce_fusion.6, f32[2048]{0:T(1024)S(1)} %get-tuple-element.225, f32[32,2048]{1,0:T(8,128)} %get-tuple-element.215, pred[]{:T(512)S(6)} %compare.6, ...), kind=kOutput, calls=%fused_computation.19.clone.1 | convolution fusion | flops 413270016 | bytes 996353 | tf_op jit(solution)/shard_map/while/body/eval_jaxpr/dot_general | solution.py:51
  148.1 4.2 %convolution_add_fusion.2 = f32[32,2048]{1,0:T(8,128)} fusion(bf16[64,2048]{1,0:T(8,128)(2,1)S(1)} %get-tuple-element.227, f32[1024]{0:T(1024)S(1)} %multiply_reduce_fusion.6, f32[2048]{0:T(1024)S(1)} %get-tuple-element.225, f32[32,2048]{1,0:T(8,128)} %get-tuple-element.215, pred[]{:T(512)S(6)} %compare.6, ...), kind=kOutput, calls=%fused_computation.19.clone.1 | convolution fusion | flops 413270016 | bytes 996353 | tf_op jit(solution)/shard_map/while/body/eval_jaxpr/dot_general | solution.py:51
  152.3 4.2 %convolution_add_fusion.2 = f32[32,2048]{1,0:T(8,128)} fusion(bf16[64,2048]{1,0:T(8,128)(2,1)S(1)} %get-tuple-element.227, f32[1024]{0:T(1024)S(1)} %multiply_reduce_fusion.6, f32[2048]{0:T(1024)S(1)} %get-tuple-element.225, f32[32,2048]{1,0:T(8,128)} %get-tuple-element.215, pred[]{:T(512)S(6)} %compare.6, ...), kind=kOutput, calls=%fused_computation.19.clone.1 | convolution fusion | flops 413270016 | bytes 996353 | tf_op jit(solution)/shard_map/while/body/eval_jaxpr/dot_general | solution.py:51
  156.5 4.2 %convolution_add_fusion.2 = f32[32,2048]{1,0:T(8,128)} fusion(bf16[64,2048]{1,0:T(8,128)(2,1)S(1)} %get-tuple-element.227, f32[1024]{0:T(1024)S(1)} %multiply_reduce_fusion.6, f32[2048]{0:T(1024)S(1)} %get-tuple-element.225, f32[32,2048]{1,0:T(8,128)} %get-tuple-element.215, pred[]{:T(512)S(6)} %compare.6, ...), kind=kOutput, calls=%fused_computation.19.clone.1 | convolution fusion | flops 413270016 | bytes 996353 | tf_op jit(solution)/shard_map/while/body/eval_jaxpr/dot_general | solution.py:51
  160.7 4.2 %convolution_add_fusion.2 = f32[32,2048]{1,0:T(8,128)} fusion(bf16[64,2048]{1,0:T(8,128)(2,1)S(1)} %get-tuple-element.227, f32[1024]{0:T(1024)S(1)} %multiply_reduce_fusion.6, f32[2048]{0:T(1024)S(1)} %get-tuple-element.225, f32[32,2048]{1,0:T(8,128)} %get-tuple-element.215, pred[]{:T(512)S(6)} %compare.6, ...), kind=kOutput, calls=%fused_computation.19.clone.1 | convolution fusion | flops 413270016 | bytes 996353 | tf_op jit(solution)/shard_map/while/body/eval_jaxpr/dot_general | solution.py:51
  164.9 4.2 %convolution_add_fusion.2 = f32[32,2048]{1,0:T(8,128)} fusion(bf16[64,2048]{1,0:T(8,128)(2,1)S(1)} %get-tuple-element.227, f32[1024]{0:T(1024)S(1)} %multiply_reduce_fusion.6, f32[2048]{0:T(1024)S(1)} %get-tuple-element.225, f32[32,2048]{1,0:T(8,128)} %get-tuple-element.215, pred[]{:T(512)S(6)} %compare.6, ...), kind=kOutput, calls=%fused_computation.19.clone.1 | convolution fusion | flops 413270016 | bytes 996353 | tf_op jit(solution)/shard_map/while/body/eval_jaxpr/dot_general | solution.py:51
  169.1 4.2 %convolution_add_fusion.2 = f32[32,2048]{1,0:T(8,128)} fusion(bf16[64,2048]{1,0:T(8,128)(2,1)S(1)} %get-tuple-element.227, f32[1024]{0:T(1024)S(1)} %multiply_reduce_fusion.6, f32[2048]{0:T(1024)S(1)} %get-tuple-element.225, f32[32,2048]{1,0:T(8,128)} %get-tuple-element.215, pred[]{:T(512)S(6)} %compare.6, ...), kind=kOutput, calls=%fused_computation.19.clone.1 | convolution fusion | flops 413270016 | bytes 996353 | tf_op jit(solution)/shard_map/while/body/eval_jaxpr/dot_general | solution.py:51
  173.4 4.2 %convolution_add_fusion.2 = f32[32,2048]{1,0:T(8,128)} fusion(bf16[64,2048]{1,0:T(8,128)(2,1)S(1)} %get-tuple-element.227, f32[1024]{0:T(1024)S(1)} %multiply_reduce_fusion.6, f32[2048]{0:T(1024)S(1)} %get-tuple-element.225, f32[32,2048]{1,0:T(8,128)} %get-tuple-element.215, pred[]{:T(512)S(6)} %compare.6, ...), kind=kOutput, calls=%fused_computation.19.clone.1 | convolution fusion | flops 413270016 | bytes 996353 | tf_op jit(solution)/shard_map/while/body/eval_jaxpr/dot_general | solution.py:51
  178.5 108.1 %while.21 = (s32[]{:T(128)}, f32[16,1024,32]{1,0,2:T(8,128)}, f32[2048]{0:T(1024)S(1)}, bf16[16,64,1024]{2,1,0:T(8,128)(2,1)S(1)}, bf16[64,2048]{1,0:T(8,128)(2,...) while((s32[]{:T(128)}, f32[16,1024,32]{1,0,2:T(8,128)}, f32[2048]{0:T(1024)S(1)}, ...), condition=%wide.region_10.11_spmd, body=%wide.region_8.10_spmd.sunk | while | flops 413334528 | bytes 1327201 | solution.py:70
  181.6 3.6 %dynamic_update_slice.5 = f32[16,1024,32]{1,0,2:T(8,128)} dynamic-update-slice(f32[16,1024,32]{1,0,2:T(8,128)} %get-tuple-element.239, f32[1,1024,32]{1,0,2:T(1,128)S(1)} %copy.32, s32[]{:T(128)} %get-tuple-element.238, s32[]{:T(128)} %constant.94.clone.1..sunk, s32[]{:T(128)} %constant.94.clone.1..sunk) | dynamic-update-slice | bytes 262148 | tf_op jit(solution)/shard_map/while/body/jit(dynamic_update_index_in_dim)/dynamic_update_slice | solution.py:70
  188.4 3.6 %dynamic_update_slice.5 = f32[16,1024,32]{1,0,2:T(8,128)} dynamic-update-slice(f32[16,1024,32]{1,0,2:T(8,128)} %get-tuple-element.239, f32[1,1024,32]{1,0,2:T(1,128)S(1)} %copy.32, s32[]{:T(128)} %get-tuple-element.238, s32[]{:T(128)} %constant.94.clone.1..sunk, s32[]{:T(128)} %constant.94.clone.1..sunk) | dynamic-update-slice | bytes 262148 | tf_op jit(solution)/shard_map/while/body/jit(dynamic_update_index_in_dim)/dynamic_update_slice | solution.py:70
  192.0 2.9 fusion.46
  195.1 3.6 %dynamic_update_slice.5 = f32[16,1024,32]{1,0,2:T(8,128)} dynamic-update-slice(f32[16,1024,32]{1,0,2:T(8,128)} %get-tuple-element.239, f32[1,1024,32]{1,0,2:T(1,128)S(1)} %copy.32, s32[]{:T(128)} %get-tuple-element.238, s32[]{:T(128)} %constant.94.clone.1..sunk, s32[]{:T(128)} %constant.94.clone.1..sunk) | dynamic-update-slice | bytes 262148 | tf_op jit(solution)/shard_map/while/body/jit(dynamic_update_index_in_dim)/dynamic_update_slice | solution.py:70
  201.8 3.6 %dynamic_update_slice.5 = f32[16,1024,32]{1,0,2:T(8,128)} dynamic-update-slice(f32[16,1024,32]{1,0,2:T(8,128)} %get-tuple-element.239, f32[1,1024,32]{1,0,2:T(1,128)S(1)} %copy.32, s32[]{:T(128)} %get-tuple-element.238, s32[]{:T(128)} %constant.94.clone.1..sunk, s32[]{:T(128)} %constant.94.clone.1..sunk) | dynamic-update-slice | bytes 262148 | tf_op jit(solution)/shard_map/while/body/jit(dynamic_update_index_in_dim)/dynamic_update_slice | solution.py:70
  208.6 3.6 %dynamic_update_slice.5 = f32[16,1024,32]{1,0,2:T(8,128)} dynamic-update-slice(f32[16,1024,32]{1,0,2:T(8,128)} %get-tuple-element.239, f32[1,1024,32]{1,0,2:T(1,128)S(1)} %copy.32, s32[]{:T(128)} %get-tuple-element.238, s32[]{:T(128)} %constant.94.clone.1..sunk, s32[]{:T(128)} %constant.94.clone.1..sunk) | dynamic-update-slice | bytes 262148 | tf_op jit(solution)/shard_map/while/body/jit(dynamic_update_index_in_dim)/dynamic_update_slice | solution.py:70
  212.2 2.9 fusion.46
  215.3 3.6 %dynamic_update_slice.5 = f32[16,1024,32]{1,0,2:T(8,128)} dynamic-update-slice(f32[16,1024,32]{1,0,2:T(8,128)} %get-tuple-element.239, f32[1,1024,32]{1,0,2:T(1,128)S(1)} %copy.32, s32[]{:T(128)} %get-tuple-element.238, s32[]{:T(128)} %constant.94.clone.1..sunk, s32[]{:T(128)} %constant.94.clone.1..sunk) | dynamic-update-slice | bytes 262148 | tf_op jit(solution)/shard_map/while/body/jit(dynamic_update_index_in_dim)/dynamic_update_slice | solution.py:70
  222.1 3.6 %dynamic_update_slice.5 = f32[16,1024,32]{1,0,2:T(8,128)} dynamic-update-slice(f32[16,1024,32]{1,0,2:T(8,128)} %get-tuple-element.239, f32[1,1024,32]{1,0,2:T(1,128)S(1)} %copy.32, s32[]{:T(128)} %get-tuple-element.238, s32[]{:T(128)} %constant.94.clone.1..sunk, s32[]{:T(128)} %constant.94.clone.1..sunk) | dynamic-update-slice | bytes 262148 | tf_op jit(solution)/shard_map/while/body/jit(dynamic_update_index_in_dim)/dynamic_update_slice | solution.py:70
  228.8 3.6 %dynamic_update_slice.5 = f32[16,1024,32]{1,0,2:T(8,128)} dynamic-update-slice(f32[16,1024,32]{1,0,2:T(8,128)} %get-tuple-element.239, f32[1,1024,32]{1,0,2:T(1,128)S(1)} %copy.32, s32[]{:T(128)} %get-tuple-element.238, s32[]{:T(128)} %constant.94.clone.1..sunk, s32[]{:T(128)} %constant.94.clone.1..sunk) | dynamic-update-slice | bytes 262148 | tf_op jit(solution)/shard_map/while/body/jit(dynamic_update_index_in_dim)/dynamic_update_slice | solution.py:70
  235.5 3.6 %dynamic_update_slice.5 = f32[16,1024,32]{1,0,2:T(8,128)} dynamic-update-slice(f32[16,1024,32]{1,0,2:T(8,128)} %get-tuple-element.239, f32[1,1024,32]{1,0,2:T(1,128)S(1)} %copy.32, s32[]{:T(128)} %get-tuple-element.238, s32[]{:T(128)} %constant.94.clone.1..sunk, s32[]{:T(128)} %constant.94.clone.1..sunk) | dynamic-update-slice | bytes 262148 | tf_op jit(solution)/shard_map/while/body/jit(dynamic_update_index_in_dim)/dynamic_update_slice | solution.py:70
  242.3 3.6 %dynamic_update_slice.5 = f32[16,1024,32]{1,0,2:T(8,128)} dynamic-update-slice(f32[16,1024,32]{1,0,2:T(8,128)} %get-tuple-element.239, f32[1,1024,32]{1,0,2:T(1,128)S(1)} %copy.32, s32[]{:T(128)} %get-tuple-element.238, s32[]{:T(128)} %constant.94.clone.1..sunk, s32[]{:T(128)} %constant.94.clone.1..sunk) | dynamic-update-slice | bytes 262148 | tf_op jit(solution)/shard_map/while/body/jit(dynamic_update_index_in_dim)/dynamic_update_slice | solution.py:70
  249.1 3.6 %dynamic_update_slice.5 = f32[16,1024,32]{1,0,2:T(8,128)} dynamic-update-slice(f32[16,1024,32]{1,0,2:T(8,128)} %get-tuple-element.239, f32[1,1024,32]{1,0,2:T(1,128)S(1)} %copy.32, s32[]{:T(128)} %get-tuple-element.238, s32[]{:T(128)} %constant.94.clone.1..sunk, s32[]{:T(128)} %constant.94.clone.1..sunk) | dynamic-update-slice | bytes 262148 | tf_op jit(solution)/shard_map/while/body/jit(dynamic_update_index_in_dim)/dynamic_update_slice | solution.py:70
  255.8 3.6 %dynamic_update_slice.5 = f32[16,1024,32]{1,0,2:T(8,128)} dynamic-update-slice(f32[16,1024,32]{1,0,2:T(8,128)} %get-tuple-element.239, f32[1,1024,32]{1,0,2:T(1,128)S(1)} %copy.32, s32[]{:T(128)} %get-tuple-element.238, s32[]{:T(128)} %constant.94.clone.1..sunk, s32[]{:T(128)} %constant.94.clone.1..sunk) | dynamic-update-slice | bytes 262148 | tf_op jit(solution)/shard_map/while/body/jit(dynamic_update_index_in_dim)/dynamic_update_slice | solution.py:70
  262.6 3.6 %dynamic_update_slice.5 = f32[16,1024,32]{1,0,2:T(8,128)} dynamic-update-slice(f32[16,1024,32]{1,0,2:T(8,128)} %get-tuple-element.239, f32[1,1024,32]{1,0,2:T(1,128)S(1)} %copy.32, s32[]{:T(128)} %get-tuple-element.238, s32[]{:T(128)} %constant.94.clone.1..sunk, s32[]{:T(128)} %constant.94.clone.1..sunk) | dynamic-update-slice | bytes 262148 | tf_op jit(solution)/shard_map/while/body/jit(dynamic_update_index_in_dim)/dynamic_update_slice | solution.py:70
  269.4 3.6 %dynamic_update_slice.5 = f32[16,1024,32]{1,0,2:T(8,128)} dynamic-update-slice(f32[16,1024,32]{1,0,2:T(8,128)} %get-tuple-element.239, f32[1,1024,32]{1,0,2:T(1,128)S(1)} %copy.32, s32[]{:T(128)} %get-tuple-element.238, s32[]{:T(128)} %constant.94.clone.1..sunk, s32[]{:T(128)} %constant.94.clone.1..sunk) | dynamic-update-slice | bytes 262148 | tf_op jit(solution)/shard_map/while/body/jit(dynamic_update_index_in_dim)/dynamic_update_slice | solution.py:70
  276.1 3.6 %dynamic_update_slice.5 = f32[16,1024,32]{1,0,2:T(8,128)} dynamic-update-slice(f32[16,1024,32]{1,0,2:T(8,128)} %get-tuple-element.239, f32[1,1024,32]{1,0,2:T(1,128)S(1)} %copy.32, s32[]{:T(128)} %get-tuple-element.238, s32[]{:T(128)} %constant.94.clone.1..sunk, s32[]{:T(128)} %constant.94.clone.1..sunk) | dynamic-update-slice | bytes 262148 | tf_op jit(solution)/shard_map/while/body/jit(dynamic_update_index_in_dim)/dynamic_update_slice | solution.py:70
  282.9 3.6 %dynamic_update_slice.5 = f32[16,1024,32]{1,0,2:T(8,128)} dynamic-update-slice(f32[16,1024,32]{1,0,2:T(8,128)} %get-tuple-element.239, f32[1,1024,32]{1,0,2:T(1,128)S(1)} %copy.32, s32[]{:T(128)} %get-tuple-element.238, s32[]{:T(128)} %constant.94.clone.1..sunk, s32[]{:T(128)} %constant.94.clone.1..sunk) | dynamic-update-slice | bytes 262148 | tf_op jit(solution)/shard_map/while/body/jit(dynamic_update_index_in_dim)/dynamic_update_slice | solution.py:70
  286.6 4.2 %copy.29 = f32[4,8,16,1024]{3,1,2,0:T(8,128)} copy(f32[4,8,16,1024]{3,2,1,0:T(8,128)} %bitcast.103) | data formatting | bytes 4194304
  290.7 60.2 %reduce-scatter.2.cloned.1.call-done = f32[1024,32]{0,1:T(8,128)} async-done(((f32[16384,32]{0,1:T(8,128)}), f32[1024,32]{0,1:T(8,128)}) %reduce-scatter.2.cloned.1.call-update) | async-done | bytes 131088 | tf_op jit(solution)/shard_map/reduce_scatter | solution.py:71
  (98 shorter events, 55.9 us)
Async XLA Ops:
  6.5 51.6 %all-gather.5.cloned.1.call-start = ((), (), s32[]{:S(2)}) async-start(), calls=%async_computation.4 | async-start | bytes 1114112 | tf_op jit(solution)/shard_map/all_gather | solution.py:43
  8.8 49.2 %copy-start = (bf16[64,2048]{1,0:T(8,128)(2,1)S(1)}, bf16[64,2048]{1,0:T(8,128)(2,1)}, u32[]{:S(2)}) copy-start(bf16[64,2048]{1,0:T(8,128)(2,1)} %param.8) | copy-start | bytes 786436
  18.7 13.8 %all-to-all-start = ((s32[16,128,1]{1,2,0:T(1,128)}), s32[16,128,1]{1,2,0:T(1,128)S(1)}, u32[]{:S(2)}, u32[]{:S(2)}) async-start(s32[16,128,1]{1,2,0:T(1,128)} %bitcast.6), calls=%async_computation | async-start | bytes 16384 | tf_op jit(solution)/shard_map/all_to_all | solution.py:35
  39.7 13.8 %all-to-all-start.1 = ((bf16[64,16,128]{2,0,1:T(8,128)(2,1)}), bf16[64,16,128]{2,0,1:T(8,128)(2,1)S(1)}, u32[]{:S(2)}, u32[]{:S(2)}) async-start(bf16[64,16,128]{2,0,1:T(8,128)(2,1)} %broadcast_select_fusion), calls=%async_computation.1 | async-start | bytes 524288 | tf_op jit(solution)/shard_map/all_to_all | solution.py:37
  43.2 64.2 %all-gather.3.cloned.1.call-start = ((), (), s32[]{:S(2)}) async-start(), calls=%async_computation.3 | async-start | bytes 4456448 | tf_op jit(solution)/shard_map/all_gather | solution.py:61
  57.9 293.0 %reduce-scatter.2.cloned.1.call-start = ((), (), s32[]{:S(2)}) async-start(), calls=%async_computation.5 | async-start | bytes 2228224 | tf_op jit(solution)/shard_map/reduce_scatter | solution.py:71
Sparse Core Ops, SparseCore 0:
  9.5 41.8 all-gather.4
  58.0 49.3 all-gather.2
  290.9 59.9 reduce-scatter.1
where the time goes:
time: 361 us; the launch traced here: 359 us
  waiting for transfers between devices  123 us (34%)
  matrix products  112 us (31%)
  local copies, waits for them, and re-layouts  87 us (24%)
  between operations  13.3 us (4%)
  other arithmetic  12.5 us (3%)
  starting transfers between devices  11 us (3%)
    dot_general x16, matrix products, step(): lax.dot_general(probe_cols, kernel, (((1,), (1,)), ((), ())), preferred_e...  65.8 us
    dynamic_update_slice x32, local copies, waits for them, and re-layouts, local(): lax.map(single, split_columns(piece, span))  60.7 us
    reduce_scatter x1, waiting for transfers between devices, local(): summed = lax.psum_scatter(terms, 'blk', scatter_dimension=0, tiled=True)  60.2 us
    all_gather x1, waiting for transfers between devices, local(): piece = lax.all_gather(centres, 'blk', axis=1, tiled=True)  46.9 us
    dot_general x16, matrix products, single(): lax.dot_general(kernel, hidden, (((0,), (1,)), ((), ())), preferred_eleme...  46.6 us
    all_to_all x1, waiting for transfers between devices, local(): lax.all_to_all(outgoing, 'blk', split_axis=1, concat_axis=1, tiled=True)  10.2 us
    unnamed x6, local copies, waits for them, and re-layouts  7.78 us
    all_to_all x1, starting transfers between devices, local(): lax.all_to_all(wanted, 'blk', split_axis=0, concat_axis=0, tiled=True)  7.39 us
  transfers between devices with their start and end apart: 5, of which 4 were waited for; matrix products, arithmetic and copies ran while one was open for 7% of the time, Pallas kernels for 0%

commit v1 on v0

v1 whole, which is shorter than its diff:
```python
import functools
import math

import jax
import jax.numpy as jnp
from jax import lax
from jax.experimental import pallas as pl
from jax.experimental.pallas import tpu as pltpu
from jax.sharding import PartitionSpec as P

LANES = 128
ROWS = 256
DEPTH = 256
STORE_BYTES = 40 * 2**20
LOG2E = math.log2(math.e)


def three_parts(value):
    high = value.astype(jnp.bfloat16)
    rest = value - high.astype(jnp.float32)
    middle = rest.astype(jnp.bfloat16)
    low = (rest - middle.astype(jnp.float32)).astype(jnp.bfloat16)
    return high, middle, low


def stack_rows(count, rows, columns):
    place = lax.broadcasted_iota(jnp.int32, (count, columns), 0)
    total = jnp.zeros((count, columns), jnp.float32)
    for at, row in enumerate(rows):
        total = jnp.where(place == at, jnp.broadcast_to(row, (count, columns)), total)
    return total


def body(
    blocks, stored, samples, index, signs, scale, out,
    xaug, caug, probe_t, hidden_t, hidden, slot_hot, wanted, asked, reply, arrived,
    pieces, kept, partial, incoming, own,
    ask_send, ask_recv, reply_send, reply_recv, piece_send, piece_recv, sum_send, sum_recv,
):
    features, s_dev = samples.shape
    m_dev = index.shape[1]
    probes = signs.shape[0]
    lines = blocks // 4
    me = lax.axis_index("blk")
    line, side, core = me // 4, (me // 2) % 2, me % 2
    f32, bf16 = jnp.float32, jnp.bfloat16

    def copy_to(peer, src, dst, send, recv):
        return pltpu.make_async_remote_copy(
            src_ref=src, dst_ref=dst, send_sem=send, recv_sem=recv,
            device_id={"blk": peer}, device_id_type=pl.DeviceIdType.MESH,
        )

    barrier = pltpu.get_barrier_semaphore()

    @pl.loop(1, blocks)
    def _(t):
        pl.semaphore_signal(
            barrier, inc=1, device_id={"blk": lax.rem(me + t, blocks)},
            device_id_type=pl.DeviceIdType.MESH,
        )

    picked = index[...]
    owner = picked // s_dev
    place = picked - owner * s_dev
    owner_hot = lax.broadcasted_iota(jnp.int32, (blocks, m_dev), 0) == owner
    owner_bf = jnp.where(owner_hot, 1.0, 0.0).astype(bf16)
    step = min(256, m_dev)
    ranks = []
    for at in range(0, m_dev, step):
        before = lax.broadcasted_iota(jnp.int32, (m_dev, step), 0) < (
            lax.broadcasted_iota(jnp.int32, (m_dev, step), 1) + at
        )
        ranks.append(
            jnp.dot(owner_bf, jnp.where(before, 1.0, 0.0).astype(bf16), preferred_element_type=f32)
        )
    rank = jnp.sum(
        jnp.where(owner_hot, jnp.concatenate(ranks, axis=1), 0.0), axis=0, keepdims=True
    )
    slot = owner * LANES + rank.astype(jnp.int32)
    digits = stack_rows(
        16, [(place // 64).astype(f32), (place % 64).astype(f32)], m_dev
    ).astype(bf16)

    def ask(peer):
        rows = pl.ds(pl.multiple_of(peer * LANES, LANES), LANES)
        hot = lax.broadcasted_iota(jnp.int32, (LANES, m_dev), 0) + peer * LANES == slot
        hot = jnp.where(hot, 1.0, 0.0).astype(bf16)
        slot_hot[rows, :] = hot
        found = lax.dot_general(digits, hot, (((1,), (1,)), ((), ())), preferred_element_type=f32)
        return jnp.broadcast_to(found[0:1] * 64.0 + found[1:2], (8, LANES))

    asked[me] = ask(me)
    pl.semaphore_wait(barrier, blocks - 1)

    @pl.loop(1, blocks)
    def _(t):
        peer = lax.rem(me + t, blocks)
        wanted[peer] = ask(peer)
        copy_to(peer, wanted.at[peer], asked.at[me], ask_send.at[peer], ask_recv.at[me]).start()

    ones = jnp.ones((1, s_dev), f32)
    points = samples[...]
    wide = points.astype(f32)
    norm = jnp.sum(wide * wide, axis=0, keepdims=True) * (-2.0 * LOG2E / features)
    parts = [part.astype(f32) for part in three_parts(norm)]
    turned = wide.T.astype(bf16)
    for at in range(3):
        xaug[:, at * features:(at + 1) * features] = turned
    rest = DEPTH - 3 * features
    xaug[:, 3 * features:] = stack_rows(rest, parts + [ones] * 3, s_dev).T.astype(bf16)
    hidden_t[...] = jnp.zeros_like(hidden_t)

    def answer(peer):
        want = asked[peer][0:1].astype(jnp.int32)
        hot = lax.broadcasted_iota(jnp.int32, (s_dev, LANES), 0) == want
        hot = jnp.where(hot, 1.0, 0.0).astype(bf16)
        return jnp.dot(points, hot, preferred_element_type=f32).astype(bf16)

    mine = pl.ds(pl.multiple_of(me * LANES, LANES), LANES)
    arrived[:, mine] = answer(me)

    @pl.loop(1, blocks)
    def _(t):
        peer = lax.rem(me - t + blocks, blocks)
        copy_to(peer, wanted.at[peer], asked.at[peer], ask_send.at[peer], ask_recv.at[peer]).wait_recv()
        reply[peer] = answer(peer)
        copy_to(
            peer, reply.at[peer], arrived.at[:, mine], reply_send.at[peer], reply_recv.at[me]
        ).start()

    probe = (2 * signs[...] - 1).astype(f32) * scale[...]
    pieces[me, features:, :] = probe.astype(bf16)

    @pl.loop(1, blocks)
    def _(t):
        peer = lax.rem(me + t, blocks)
        theirs = pl.ds(pl.multiple_of(peer * LANES, LANES), LANES)
        copy_to(
            peer, reply.at[peer], arrived.at[:, theirs], reply_send.at[peer], reply_recv.at[peer]
        ).wait_recv()

    pieces[me, :features, :] = jnp.dot(
        arrived[...], slot_hot[...], preferred_element_type=f32
    ).astype(bf16)

    def holder(back, flip_side, flip_core):
        return (
            lax.rem(line - back + lines, lines) * 4
            + lax.rem(side + flip_side, 2) * 2
            + lax.rem(core + flip_core, 2)
        )

    def send_piece(piece, peer, at):
        return copy_to(
            peer, pieces.at[piece], pieces.at[piece], piece_send.at[at], piece_recv.at[piece]
        )

    def prepare(piece):
        c = pieces[piece, :features, :].astype(f32)
        for at, part in enumerate(three_parts(c * (4.0 * LOG2E / features))):
            caug[at * features:(at + 1) * features, :] = part
        square = jnp.sum(c * c, axis=0, keepdims=True) * (-2.0 * LOG2E / features)
        parts = [part.astype(f32) for part in three_parts(square)]
        ones = jnp.ones((1, m_dev), f32)
        caug[3 * features:, :] = stack_rows(rest, [ones] * 3 + parts, m_dev).astype(bf16)

    def kernel_rows(rows):
        power = jnp.dot(xaug[rows, :], caug[...], preferred_element_type=f32)
        return jnp.exp2(power).astype(bf16)

    def first(piece, at):
        prepare(piece)
        probe_t[...] = pieces[piece, features:, :].astype(f32).T.astype(bf16)

        @pl.loop(0, s_dev // ROWS)
        def _(tile):
            rows = pl.ds(pl.multiple_of(tile * ROWS, ROWS), ROWS)
            kernel = kernel_rows(rows)

            @pl.when(at < stored)
            def _():
                kept[lax.rem(at, stored), rows, :] = kernel

            hidden_t[rows, :] += jnp.dot(kernel, probe_t[...], preferred_element_type=f32)

    @pl.loop(0, lines)
    def _(back):
        held = holder(back, 0, 0)

        @pl.when(back > 0)
        def _():
            send_piece(held, held, 0).wait_recv()

        @pl.when(back < lines - 1)
        def _():
            send_piece(held, holder(lines - 1, 0, 0), back * 4).start()

        send_piece(held, holder(0, 1, 0), back * 4 + 1).start()
        send_piece(held, holder(0, 0, 1), back * 4 + 2).start()
        first(held, back * 4)
        near = holder(back, 0, 1)
        send_piece(near, near, 0).wait_recv()
        first(near, back * 4 + 1)
        across = holder(back, 1, 0)
        send_piece(across, across, 0).wait_recv()
        send_piece(across, holder(0, 0, 1), back * 4 + 3).start()
        first(across, back * 4 + 2)
        last = holder(back, 1, 1)
        send_piece(last, last, 0).wait_recv()
        first(last, back * 4 + 3)

    hidden[...] = hidden_t[...].T.astype(bf16)

    def second(at):
        def from_store():
            return jnp.dot(hidden[...], kept[at], preferred_element_type=f32)

        return from_store()

    def holder_at(at):
        return holder(at // 4, lax.rem(at // 2, 2), lax.rem(at, 2))

    def send_sum(peer):
        copy_to(peer, partial.at[peer], incoming.at[me], sum_send.at[peer], sum_recv.at[me]).start()

    @pl.loop(0, blocks - stored)
    def _(t):
        peer = holder_at(blocks - 1 - t)
        prepare(peer)
        own[...] = jnp.zeros_like(own)

        @pl.loop(0, s_dev // ROWS)
        def _(tile):
            rows = pl.ds(pl.multiple_of(tile * ROWS, ROWS), ROWS)
            own[...] += jnp.dot(hidden[:, rows], kernel_rows(rows), preferred_element_type=f32)

        partial[peer] = own[...].astype(bf16)
        send_sum(peer)

    @pl.loop(0, stored - 1)
    def _(t):
        at = stored - 1 - t
        peer = holder_at(at)
        partial[peer] = second(at).astype(bf16)
        send_sum(peer)

    own[...] = second(0)

    @pl.loop(1, blocks)
    def _(t):
        peer = lax.rem(me + t, blocks)
        copy_to(peer, partial.at[peer], incoming.at[peer], sum_send.at[peer], sum_recv.at[peer]).wait()
        own[...] += incoming[peer].astype(f32)

    out[...] = (own[...] * (1.0 / (s_dev * blocks))).T

    @pl.loop(1, blocks)
    def _(t):
        peer = lax.rem(me + t, blocks)
        copy_to(peer, wanted.at[peer], asked.at[peer], ask_send.at[peer], ask_recv.at[peer]).wait_send()
        copy_to(
            peer, reply.at[peer], arrived.at[:, mine], reply_send.at[peer], reply_recv.at[peer]
        ).wait_send()

    @pl.loop(0, lines)
    def _(back):
        @pl.when(back < lines - 1)
        def _():
            send_piece(me, holder(lines - 1, 0, 0), back * 4).wait_send()

        send_piece(me, holder(0, 1, 0), back * 4 + 1).wait_send()
        send_piece(me, holder(0, 0, 1), back * 4 + 2).wait_send()
        send_piece(me, holder(0, 0, 1), back * 4 + 3).wait_send()


def local(samples, centre_index, probe_signs, probe_scale):
    blocks = lax.axis_size("blk")
    features, s_dev = samples.shape
    m_dev = centre_index.shape[0]
    probes = probe_signs.shape[0]
    f32, bf16 = jnp.float32, jnp.bfloat16
    stored = min(blocks, STORE_BYTES // (s_dev * m_dev * 2))
    vmem = pl.BlockSpec(memory_space=pltpu.VMEM)
    return pl.pallas_call(
        functools.partial(body, blocks, stored),
        out_shape=jax.ShapeDtypeStruct((m_dev, probes), f32),
        in_specs=[vmem] * 4,
        out_specs=vmem,
        scratch_shapes=[
            pltpu.VMEM((s_dev, DEPTH), bf16),
            pltpu.VMEM((DEPTH, m_dev), bf16),
            pltpu.VMEM((m_dev, probes), bf16),
            pltpu.VMEM((s_dev, probes), f32),
            pltpu.VMEM((probes, s_dev), bf16),
            pltpu.VMEM((blocks * LANES, m_dev), bf16),
            pltpu.VMEM((blocks, 8, LANES), f32),
            pltpu.VMEM((blocks, 8, LANES), f32),
            pltpu.VMEM((blocks, features, LANES), bf16),
            pltpu.VMEM((features, blocks * LANES), bf16),
            pltpu.VMEM((blocks, features + probes, m_dev), bf16),
            pltpu.VMEM((stored, s_dev, m_dev), bf16),
            pltpu.VMEM((blocks, probes, m_dev), bf16),
            pltpu.VMEM((blocks, probes, m_dev), bf16),
            pltpu.VMEM((probes, m_dev), f32),
        ] + [pltpu.SemaphoreType.DMA((blocks,))] * 8,
        compiler_params=pltpu.CompilerParams(
            collective_id=0, has_side_effects=True, vmem_limit_bytes=62 * 2**20
        ),
    )(samples, centre_index[None, :], probe_signs, probe_scale[None, :])


def solution(mesh):
    in_specs = (
        P(None, ("groups", "blk")),
        P(("groups", "blk")),
        P(None, ("groups", "blk")),
        P(("groups", "blk")),
    )
    out_specs = P(("groups", "blk"), None)
    return jax.shard_map(local, mesh=mesh, in_specs=in_specs, out_specs=out_specs, check_vma=False)
```

time: 361 us -> 145 us (0.40)
  Pallas kernels: 0 us -> 142 us
  waiting for transfers between devices: 123 us -> 0 us
  matrix products: 112 us -> 0 us
  local copies, waits for them, and re-layouts: 87 us -> 1.87 us
  between operations: 13.3 us -> 0.01 us
  other arithmetic: 12.5 us -> 0 us
  starting transfers between devices: 11 us -> 0 us
    pallas_call x0 -> x1, Pallas kernels: none -> 142 us  [local(): pl.pallas_call(functools.partial(body, blocks, stored), out_shape=jax.Sha...]
    dot_general x32 -> x0, matrix products: 112 us -> none  [the longest x16 65.8 us: step(): lax.dot_general(probe_cols, kernel, (((1,), (1,)), ((), ())), preferred_e...]
    dynamic_update_slice x32 -> x0, local copies, waits for them, and re-layouts: 60.7 us -> none  [local(): lax.map(single, split_columns(piece, span))]
    reduce_scatter x1 -> x0, waiting for transfers between devices: 60.2 us -> none  [local(): summed = lax.psum_scatter(terms, 'blk', scatter_dimension=0, tiled=True)]
    all_gather x2 -> x0, waiting for transfers between devices: 47 us -> none  [the longest x1 46.9 us: local(): piece = lax.all_gather(centres, 'blk', axis=1, tiled=True)]
    all_to_all x2 -> x0, waiting for transfers between devices: 15.4 us -> none  [the longest x1 10.2 us: local(): lax.all_to_all(outgoing, 'blk', split_axis=1, concat_axis=1, tiled=True)]
    all_to_all x2 -> x0, starting transfers between devices: 10.9 us -> none  [the longest x1 7.39 us: local(): lax.all_to_all(wanted, 'blk', split_axis=0, concat_axis=0, tiled=True)]
    gather x3 -> x0, local copies, waits for them, and re-layouts: 9.61 us -> none  [the longest x2 6.4 us: local(): outgoing = jnp.take(samples, asked, axis=1)]
  transfers between devices with their start and end apart: 5 -> 0, of which waited for: 4 -> 0; matrix products, arithmetic and copies ran while one was open for 7% -> 0% of each run, Pallas kernels for 0% -> 0%
where the time goes in v1:
time: 145 us; the launch traced here: 143 us
  Pallas kernels  142 us (98%)
  local copies, waits for them, and re-layouts  1.87 us (1%)
    pallas_call x1, Pallas kernels, local(): pl.pallas_call(functools.partial(body, blocks, stored), out_shape=jax.Sha...  142 us

profile of v1, /device:TPU:0, one launch (start us, length us, event | category | flops | bytes accessed | tf_op | source)
XLA Modules:
  0.0 143.4 jit_solution(5778169156748159469)
XLA Ops:
  0.0 141.5 %shard_map.46 = f32[1024,32]{1,0:T(8,128)} custom-call(bf16[64,2048]{1,0:T(8,128)(2,1)} %samples.1, s32[1,1024]{1,0:T(1,128)} %bitcast.2, s32[32,1024]{1,0:T(8,128)} %signs.1, f32[1,1024]{1,0:T(1,128)} %bitcast.3), custom_call_target="tpu_custom_call" | custom-call | tf_op jit(solution)/shard_map/pallas_call | solution.py:285
  141.6 1.9 %copy.5 = f32[1024,32]{0,1:T(8,128)} copy(f32[1024,32]{1,0:T(8,128)} %shard_map.46) | data formatting | bytes 262144 | tf_op jit(solution)/shard_map/pallas_call | solution.py:285

commit v2 on v1

--- a/solution.py
+++ b/solution.py
@@ -9,9 +9,9 @@
 from jax.sharding import PartitionSpec as P
 
 LANES = 128
-ROWS = 256
+ROWS = 2048
 DEPTH = 256
-STORE_BYTES = 40 * 2**20
+STORE_BYTES = 32 * 2**20
 LOG2E = math.log2(math.e)
 
 
@@ -33,9 +33,10 @@
 
 def body(
     blocks, stored, samples, index, signs, scale, out,
-    xaug, caug, probe_t, hidden_t, hidden, slot_hot, wanted, asked, reply, arrived,
-    pieces, kept, partial, incoming, own,
-    ask_send, ask_recv, reply_send, reply_recv, piece_send, piece_recv, sum_send, sum_recv,
+    xaug, caug, hidden_t, hidden, slot_hot, wanted, asked, reply, arrived,
+    pieces, kept, partial, from_twin, incoming, own,
+    ask_send, ask_recv, reply_send, reply_recv, piece_send, piece_recv,
+    twin_send, twin_recv, sum_send, sum_recv,
 ):
     features, s_dev = samples.shape
     m_dev = index.shape[1]
@@ -44,6 +45,8 @@
     me = lax.axis_index("blk")
     line, side, core = me // 4, (me // 2) % 2, me % 2
     f32, bf16 = jnp.float32, jnp.bfloat16
+    if blocks * LANES == s_dev:
+        slot_hot = kept.at[stored]
 
     def copy_to(peer, src, dst, send, recv):
         return pltpu.make_async_remote_copy(
@@ -171,18 +174,17 @@
 
     def first(piece, at):
         prepare(piece)
-        probe_t[...] = pieces[piece, features:, :].astype(f32).T.astype(bf16)
 
         @pl.loop(0, s_dev // ROWS)
         def _(tile):
             rows = pl.ds(pl.multiple_of(tile * ROWS, ROWS), ROWS)
             kernel = kernel_rows(rows)
 
-            @pl.when(at < stored)
-            def _():
-                kept[lax.rem(at, stored), rows, :] = kernel
-
-            hidden_t[rows, :] += jnp.dot(kernel, probe_t[...], preferred_element_type=f32)
+            kept[lax.min(at, stored), rows, :] = kernel
+            hidden_t[:, rows] += lax.dot_general(
+                pieces[piece, features:, :], kernel, (((1,), (1,)), ((), ())),
+                preferred_element_type=f32,
+            )
 
     @pl.loop(0, lines)
     def _(back):
@@ -210,24 +212,37 @@
         send_piece(last, last, 0).wait_recv()
         first(last, back * 4 + 3)
 
-    hidden[...] = hidden_t[...].T.astype(bf16)
-
-    def second(at):
-        def from_store():
-            return jnp.dot(hidden[...], kept[at], preferred_element_type=f32)
-
-        return from_store()
+    hidden[...] = hidden_t[...].astype(bf16)
 
     def holder_at(at):
         return holder(at // 4, lax.rem(at // 2, 2), lax.rem(at, 2))
 
-    def send_sum(peer):
-        copy_to(peer, partial.at[peer], incoming.at[me], sum_send.at[peer], sum_recv.at[me]).start()
-
-    @pl.loop(0, blocks - stored)
-    def _(t):
-        peer = holder_at(blocks - 1 - t)
-        prepare(peer)
+    twin = holder(0, 0, 1)
+
+    def send_twin(pair):
+        return copy_to(
+            twin, partial.at[2 * pair + 1], from_twin.at[pair],
+            twin_send.at[pair], twin_recv.at[pair],
+        )
+
+    def send_sum(pair, peer, slot):
+        return copy_to(
+            peer, partial.at[2 * pair], incoming.at[slot], sum_send.at[pair], sum_recv.at[slot]
+        )
+
+    def both(pair, product):
+        partial[2 * pair + 1] = product(2 * pair + 1).astype(bf16)
+        send_twin(pair).start()
+        total = product(2 * pair)
+        send_twin(pair).wait_recv()
+        return total + from_twin[pair].astype(f32)
+
+    def forward(pair, total):
+        partial[2 * pair] = total.astype(bf16)
+        send_sum(pair, holder_at(2 * pair), me // 2).start()
+
+    def again(at):
+        prepare(holder_at(at))
         own[...] = jnp.zeros_like(own)
 
         @pl.loop(0, s_dev // ROWS)
@@ -235,23 +250,30 @@
             rows = pl.ds(pl.multiple_of(tile * ROWS, ROWS), ROWS)
             own[...] += jnp.dot(hidden[:, rows], kernel_rows(rows), preferred_element_type=f32)
 
-        partial[peer] = own[...].astype(bf16)
-        send_sum(peer)
-
-    @pl.loop(0, stored - 1)
-    def _(t):
-        at = stored - 1 - t
-        peer = holder_at(at)
-        partial[peer] = second(at).astype(bf16)
-        send_sum(peer)
-
-    own[...] = second(0)
-
-    @pl.loop(1, blocks)
-    def _(t):
-        peer = lax.rem(me + t, blocks)
-        copy_to(peer, partial.at[peer], incoming.at[peer], sum_send.at[peer], sum_recv.at[peer]).wait()
-        own[...] += incoming[peer].astype(f32)
+        return own[...]
+
+    def from_store(at):
+        return jnp.dot(hidden[...], kept[at], preferred_element_type=f32)
+
+    pairs, stored_pairs = blocks // 2, stored // 2
+
+    @pl.loop(0, pairs - stored_pairs)
+    def _(t):
+        pair = pairs - 1 - t
+        forward(pair, both(pair, again))
+
+    @pl.loop(0, stored_pairs - 1)
+    def _(t):
+        pair = stored_pairs - 1 - t
+        forward(pair, both(pair, from_store))
+
+    own[...] = both(0, from_store)
+
+    @pl.loop(1, pairs)
+    def _(pair):
+        slot = holder_at(2 * pair) // 2
+        send_sum(pair, me, slot).wait_recv()
+        own[...] += incoming[slot].astype(f32)
 
     out[...] = (own[...] * (1.0 / (s_dev * blocks))).T
 
@@ -262,6 +284,13 @@
         copy_to(
             peer, reply.at[peer], arrived.at[:, mine], reply_send.at[peer], reply_recv.at[peer]
         ).wait_send()
+
+    send_twin(0).wait_send()
+
+    @pl.loop(1, pairs)
+    def _(pair):
+        send_twin(pair).wait_send()
+        send_sum(pair, me, pair).wait_send()
 
     @pl.loop(0, lines)
     def _(back):
@@ -280,7 +309,7 @@
     m_dev = centre_index.shape[0]
     probes = probe_signs.shape[0]
     f32, bf16 = jnp.float32, jnp.bfloat16
-    stored = min(blocks, STORE_BYTES // (s_dev * m_dev * 2))
+    stored = min(blocks, STORE_BYTES // (s_dev * m_dev * 2)) // 2 * 2
     vmem = pl.BlockSpec(memory_space=pltpu.VMEM)
     return pl.pallas_call(
         functools.partial(body, blocks, stored),
@@ -290,20 +319,20 @@
         scratch_shapes=[
             pltpu.VMEM((s_dev, DEPTH), bf16),
             pltpu.VMEM((DEPTH, m_dev), bf16),
-            pltpu.VMEM((m_dev, probes), bf16),
-            pltpu.VMEM((s_dev, probes), f32),
+            pltpu.VMEM((probes, s_dev), f32),
             pltpu.VMEM((probes, s_dev), bf16),
-            pltpu.VMEM((blocks * LANES, m_dev), bf16),
+            pltpu.VMEM((16 if blocks * LANES == s_dev else blocks * LANES, m_dev), bf16),
             pltpu.VMEM((blocks, 8, LANES), f32),
             pltpu.VMEM((blocks, 8, LANES), f32),
             pltpu.VMEM((blocks, features, LANES), bf16),
             pltpu.VMEM((features, blocks * LANES), bf16),
             pltpu.VMEM((blocks, features + probes, m_dev), bf16),
-            pltpu.VMEM((stored, s_dev, m_dev), bf16),
+            pltpu.VMEM((stored + 1, s_dev, m_dev), bf16),
             pltpu.VMEM((blocks, probes, m_dev), bf16),
-            pltpu.VMEM((blocks, probes, m_dev), bf16),
+            pltpu.VMEM((blocks // 2, probes, m_dev), bf16),
+            pltpu.VMEM((blocks // 2, probes, m_dev), bf16),
             pltpu.VMEM((probes, m_dev), f32),
-        ] + [pltpu.SemaphoreType.DMA((blocks,))] * 8,
+        ] + [pltpu.SemaphoreType.DMA((blocks,))] * 10,
         compiler_params=pltpu.CompilerParams(
             collective_id=0, has_side_effects=True, vmem_limit_bytes=62 * 2**20
         ),

time: 145 us -> 92.5 us (0.64)
  Pallas kernels: 142 us -> 90.4 us
    pallas_call x1, Pallas kernels: 142 us -> 90.4 us  [local(): pl.pallas_call(functools.partial(body, blocks, stored), out_shape=jax.Sha...]
where the time goes in v2:
time: 92.5 us; the launch traced here: 92.3 us
  Pallas kernels  90.4 us (98%)
  local copies, waits for them, and re-layouts  1.87 us (2%)
    pallas_call x1, Pallas kernels, local(): pl.pallas_call(functools.partial(body, blocks, stored), out_shape=jax.Sha...  90.4 us
    pallas_call x1, local copies, waits for them, and re-layouts, local(): pl.pallas_call(functools.partial(body, blocks, stored), out_shape=jax.Sha...  1.87 us

profile of v2, /device:TPU:0, one launch (start us, length us, event | category | flops | bytes accessed | tf_op | source)
XLA Modules:
  0.0 92.3 jit_solution(17688461055065871004)
XLA Ops:
  0.0 90.4 %shard_map.46 = f32[1024,32]{1,0:T(8,128)} custom-call(bf16[64,2048]{1,0:T(8,128)(2,1)} %samples.1, s32[1,1024]{1,0:T(1,128)} %bitcast.2, s32[32,1024]{1,0:T(8,128)} %signs.1, f32[1,1024]{1,0:T(1,128)} %bitcast.3), custom_call_target="tpu_custom_call" | custom-call | tf_op jit(solution)/shard_map/pallas_call | solution.py:314
  90.5 1.9 %copy.5 = f32[1024,32]{0,1:T(8,128)} copy(f32[1024,32]{1,0:T(8,128)} %shard_map.46) | data formatting | bytes 262144 | tf_op jit(solution)/shard_map/pallas_call | solution.py:314

commit v3 on v2

--- a/solution.py
+++ b/solution.py
@@ -9,9 +9,9 @@
 from jax.sharding import PartitionSpec as P
 
 LANES = 128
-ROWS = 2048
+ROWS = 1024
 DEPTH = 256
-STORE_BYTES = 32 * 2**20
+STORE_BYTES = 40 * 2**20
 LOG2E = math.log2(math.e)
 
 
@@ -85,21 +85,21 @@
         16, [(place // 64).astype(f32), (place % 64).astype(f32)], m_dev
     ).astype(bf16)
 
-    def ask(peer):
-        rows = pl.ds(pl.multiple_of(peer * LANES, LANES), LANES)
-        hot = lax.broadcasted_iota(jnp.int32, (LANES, m_dev), 0) + peer * LANES == slot
-        hot = jnp.where(hot, 1.0, 0.0).astype(bf16)
-        slot_hot[rows, :] = hot
-        found = lax.dot_general(digits, hot, (((1,), (1,)), ((), ())), preferred_element_type=f32)
-        return jnp.broadcast_to(found[0:1] * 64.0 + found[1:2], (8, LANES))
-
-    asked[me] = ask(me)
+    for at in range(0, blocks * LANES, 512):
+        hot = lax.broadcasted_iota(jnp.int32, (512, m_dev), 0) + at == slot
+        slot_hot[at:at + 512, :] = jnp.where(hot, 1.0, 0.0).astype(bf16)
+    found = lax.dot_general(
+        digits, slot_hot[...], (((1,), (1,)), ((), ())), preferred_element_type=f32
+    )
+    found = found[0:1] * 64.0 + found[1:2]
+    for peer in range(blocks):
+        wanted[peer] = jnp.broadcast_to(found[:, peer * LANES:(peer + 1) * LANES], (8, LANES))
+    asked[me] = wanted[me]
     pl.semaphore_wait(barrier, blocks - 1)
 
     @pl.loop(1, blocks)
     def _(t):
         peer = lax.rem(me + t, blocks)
-        wanted[peer] = ask(peer)
         copy_to(peer, wanted.at[peer], asked.at[me], ask_send.at[peer], ask_recv.at[me]).start()
 
     ones = jnp.ones((1, s_dev), f32)
@@ -114,23 +114,34 @@
     xaug[:, 3 * features:] = stack_rows(rest, parts + [ones] * 3, s_dev).T.astype(bf16)
     hidden_t[...] = jnp.zeros_like(hidden_t)
 
-    def answer(peer):
-        want = asked[peer][0:1].astype(jnp.int32)
-        hot = lax.broadcasted_iota(jnp.int32, (s_dev, LANES), 0) == want
+    mine = pl.ds(pl.multiple_of(me * LANES, LANES), LANES)
+    group = 4
+
+    @pl.loop(0, blocks // group)
+    def _(step):
+        peers = [lax.rem(me - step * group - t + blocks, blocks) for t in range(group)]
+        for t, peer in enumerate(peers):
+            @pl.when(step * group + t > 0)
+            def _(peer=peer):
+                copy_to(
+                    peer, wanted.at[peer], asked.at[peer], ask_send.at[peer], ask_recv.at[peer]
+                ).wait_recv()
+
+        want = jnp.concatenate([asked[peer][0:1] for peer in peers], axis=1).astype(jnp.int32)
+        hot = lax.broadcasted_iota(jnp.int32, (s_dev, group * LANES), 0) == want
         hot = jnp.where(hot, 1.0, 0.0).astype(bf16)
-        return jnp.dot(points, hot, preferred_element_type=f32).astype(bf16)
-
-    mine = pl.ds(pl.multiple_of(me * LANES, LANES), LANES)
-    arrived[:, mine] = answer(me)
-
-    @pl.loop(1, blocks)
-    def _(t):
-        peer = lax.rem(me - t + blocks, blocks)
-        copy_to(peer, wanted.at[peer], asked.at[peer], ask_send.at[peer], ask_recv.at[peer]).wait_recv()
-        reply[peer] = answer(peer)
-        copy_to(
-            peer, reply.at[peer], arrived.at[:, mine], reply_send.at[peer], reply_recv.at[me]
-        ).start()
+        chosen = jnp.dot(points, hot, preferred_element_type=f32).astype(bf16)
+        for t, peer in enumerate(peers):
+            reply[peer] = chosen[:, t * LANES:(t + 1) * LANES]
+
+            @pl.when(step * group + t > 0)
+            def _(peer=peer):
+                copy_to(
+                    peer, reply.at[peer], arrived.at[:, mine],
+                    reply_send.at[peer], reply_recv.at[me],
+                ).start()
+
+    arrived[:, mine] = reply[me]
 
     probe = (2 * signs[...] - 1).astype(f32) * scale[...]
     pieces[me, features:, :] = probe.astype(bf16)
@@ -175,7 +186,7 @@
     def first(piece, at):
         prepare(piece)
 
-        @pl.loop(0, s_dev // ROWS)
+        @pl.loop(0, s_dev // ROWS, unroll=2)
         def _(tile):
             rows = pl.ds(pl.multiple_of(tile * ROWS, ROWS), ROWS)
             kernel = kernel_rows(rows)
@@ -245,7 +256,7 @@
         prepare(holder_at(at))
         own[...] = jnp.zeros_like(own)
 
-        @pl.loop(0, s_dev // ROWS)
+        @pl.loop(0, s_dev // ROWS, unroll=2)
         def _(tile):
             rows = pl.ds(pl.multiple_of(tile * ROWS, ROWS), ROWS)
             own[...] += jnp.dot(hidden[:, rows], kernel_rows(rows), preferred_element_type=f32)
@@ -275,7 +286,7 @@
         send_sum(pair, me, slot).wait_recv()
         own[...] += incoming[slot].astype(f32)
 
-    out[...] = (own[...] * (1.0 / (s_dev * blocks))).T
+    out[...] = own[...] * (1.0 / (s_dev * blocks))
 
     @pl.loop(1, blocks)
     def _(t):
@@ -313,7 +324,7 @@
     vmem = pl.BlockSpec(memory_space=pltpu.VMEM)
     return pl.pallas_call(
         functools.partial(body, blocks, stored),
-        out_shape=jax.ShapeDtypeStruct((m_dev, probes), f32),
+        out_shape=jax.ShapeDtypeStruct((probes, m_dev), f32),
         in_specs=[vmem] * 4,
         out_specs=vmem,
         scratch_shapes=[
@@ -336,7 +347,7 @@
         compiler_params=pltpu.CompilerParams(
             collective_id=0, has_side_effects=True, vmem_limit_bytes=62 * 2**20
         ),
-    )(samples, centre_index[None, :], probe_signs, probe_scale[None, :])
+    )(samples, centre_index[None, :], probe_signs, probe_scale[None, :]).T
 
 
 def solution(mesh):

time: 92.5 us -> 90.2 us (0.975)
  Pallas kernels: 90.4 us -> 88.5 us
    pallas_call x1, Pallas kernels: 90.4 us -> 88.5 us  [local(): pl.pallas_call(functools.partial(body, blocks, stored), out_shape=jax.Sha...]
    pallas_call x1 -> x0, local copies, waits for them, and re-layouts: 1.87 us -> none  [local(): pl.pallas_call(functools.partial(body, blocks, stored), out_shape=jax.Sha...]
    unnamed x0 -> x1, local copies, waits for them, and re-layouts: none -> 1.57 us
where the time goes in v3:
time: 90.2 us; the launch traced here: 90.1 us
  Pallas kernels  88.5 us (98%)
  local copies, waits for them, and re-layouts  1.57 us (2%)
    pallas_call x1, Pallas kernels, local(): pl.pallas_call(functools.partial(body, blocks, stored), out_shape=jax.Sha...  88.5 us

profile of v3, /device:TPU:0, one launch (start us, length us, event | category | flops | bytes accessed | tf_op | source)
XLA Modules:
  0.0 90.1 jit_solution(3866717197340172687)
XLA Ops:
  0.0 88.5 %shard_map.46 = f32[32,1024]{1,0:T(8,128)} custom-call(bf16[64,2048]{1,0:T(8,128)(2,1)} %samples.1, s32[1,1024]{1,0:T(1,128)} %bitcast.4, s32[32,1024]{1,0:T(8,128)} %signs.1, f32[1,1024]{1,0:T(1,128)} %bitcast.5), custom_call_target="tpu_custom_call" | custom-call | tf_op jit(solution)/shard_map/pallas_call | solution.py:325
  88.5 1.6 %copy.6 = f32[1024,32]{0,1:T(8,128)} copy(f32[1024,32]{0,1:T(8,128)} %bitcast.3) | data formatting | bytes 262144
